TPU v7x, 512 devices: a whole 4x8x8 slice. The times are simulated.
512 devices in a mesh: fsdp: 32 (over y, z_hi), tp: 16 (over x, z_lo, core).
Axes of the slice: x: 4, y: 8, z: 8 (z_hi: 4, z_lo: 2; z = z_hi * 2 + z_lo), core: 2. Of those that a mesh axis runs over, the one named last changes fastest.
Arguments:
- acts: bfloat16 [8192, 4096], P('fsdp'), may hold values from -6 to 6
- cots: bfloat16 [8192, 14336], P('fsdp', 'tp'), may hold values from -6 to 6
- weight: bfloat16 [4096, 14336], P('fsdp', 'tp'), may hold values from -0.09375 to 0.09375
- basis_in: bfloat16 [32, 128, 128], P('fsdp'), may hold values from -0.5 to 0.5
- basis_out: bfloat16 [16, 896, 896], P('tp', 'fsdp'), may hold values from -0.1875 to 0.1875
- eigen_in: float32 [4096], P('fsdp'), may hold values from 0.2 to 5
- eigen_out: float32 [14336], P('tp'), may hold values from 0.2 to 5
- forget_rows: int32 [2048], P('fsdp'), may hold values from 0 to 255
- retain_rows: int32 [1024], P('fsdp'), may hold values from 0 to 255
Outputs:
- retained: bfloat16 [1024, 14336], P('fsdp', 'tp')
- back_grads: bfloat16 [1024, 4096], P('fsdp')
All inputs are finite; a program needn't handle non-finite values.
Results may differ from a plain program's by a relative error of at most 0.022.
Values may be sent and summed in bfloat16 or wider, within the bound.
A program may use at most 64 MiB of HBM per device.

v0:
```python
import jax
import jax.numpy as jnp
from jax import lax
from jax.sharding import PartitionSpec as P

damping = 0.1
step_size = 0.5


def shards(acts, cots, weight, basis_in, basis_out, eigen_in, eigen_out, forget_rows, retain_rows):
    fsdp_count = lax.axis_size("fsdp")
    forget_local = forget_rows.shape[0]
    forget_count = forget_local * fsdp_count
    row_count = weight.shape[0]
    col_count = weight.shape[1]
    in_blocks = basis_in.shape[0]
    in_order = basis_in.shape[1]
    forget_acts = jnp.take(acts, forget_rows, axis=0)
    forget_cots = jnp.take(cots, forget_rows, axis=0)
    basis_full = lax.all_gather(basis_out, "fsdp", axis=1, tiled=True)
    out_blocks = basis_full.shape[0]
    out_order = basis_full.shape[2]
    rotated_cots = (
        jnp.einsum(
            "tgi,gij->tgj",
            forget_cots.reshape(forget_local, out_blocks, out_order),
            basis_full,
            preferred_element_type=jnp.float32,
        )
        .reshape(forget_local, col_count)
        .astype(jnp.bfloat16)
    )
    feature_cols = lax.all_to_all(forget_acts, "fsdp", split_axis=1, concat_axis=0, tiled=True)
    rotated_acts = (
        jnp.einsum(
            "tbi,bij->tbj",
            feature_cols.reshape(forget_count, in_blocks, in_order),
            basis_in,
            preferred_element_type=jnp.float32,
        )
        .reshape(forget_count, row_count)
        .astype(jnp.bfloat16)
    )
    moments = (
        lax.dot_general(
            rotated_acts,
            lax.all_gather(rotated_cots, "fsdp", axis=0, tiled=True),
            (((0,), (0,)), ((), ())),
            preferred_element_type=jnp.float32,
        )
        / forget_count
    )
    damped = eigen_in[:, None] * eigen_out[None, :] + damping
    scaled = (moments / damped).astype(jnp.bfloat16)
    back_out = (
        jnp.einsum(
            "dgi,gji->dgj",
            scaled.reshape(row_count, out_blocks, out_order),
            basis_full,
            preferred_element_type=jnp.float32,
        )
        .reshape(row_count, col_count)
        .astype(jnp.bfloat16)
    )
    update = jnp.einsum(
        "bij,bjc->bic",
        basis_in,
        back_out.reshape(in_blocks, in_order, col_count),
        preferred_element_type=jnp.float32,
    ).reshape(row_count, col_count)
    new_weight = (weight.astype(jnp.float32) + step_size * update).astype(jnp.bfloat16)
    retain_acts = jnp.take(acts, retain_rows, axis=0)
    retain_cots = jnp.take(cots, retain_rows, axis=0)
    retain_cols = lax.all_to_all(retain_acts, "fsdp", split_axis=1, concat_axis=0, tiled=True)
    retained = lax.psum_scatter(
        jnp.dot(retain_cols, new_weight, preferred_element_type=jnp.float32).astype(jnp.bfloat16),
        "fsdp",
        scatter_dimension=0,
        tiled=True,
    )
    grad_cols = lax.dot_general(
        lax.all_gather(retain_cots, "fsdp", axis=0, tiled=True),
        new_weight,
        (((1,), (1,)), ((), ())),
        preferred_element_type=jnp.float32,
    )
    grad_summed = lax.psum(grad_cols.astype(jnp.bfloat16), "tp")
    back_grads = lax.all_to_all(grad_summed, "fsdp", split_axis=0, concat_axis=1, tiled=True)
    return (retained, back_grads)


def solution(mesh):
    placed = (
        P("fsdp", None),
        P("fsdp", "tp"),
        P("fsdp", "tp"),
        P("fsdp", None, None),
        P("tp", "fsdp", None),
        P("fsdp"),
        P("tp"),
        P("fsdp"),
        P("fsdp"),
    )
    return jax.shard_map(
        shards,
        mesh=mesh,
        in_specs=placed,
        out_specs=(P("fsdp", "tp"), P("fsdp", None)),
        check_vma=False,
    )
```

profile of v0, /device:TPU:2, one launch (start us, length us, event | category | flops | bytes accessed | tf_op | source)
XLA Modules:
  0.0 666.9 jit_solution(1411980744719282719)
XLA Ops:
  7.2 0.0 copy-start
  7.2 0.0 copy-start.1
  7.2 0.0 copy-start.5
  7.2 0.0 all-gather.4.cloned.1.call-start
  7.2 1.7 copy.25
  8.9 0.0 all-gather.4.cloned.1.call-update
  9.0 0.0 all-gather.6.cloned.1.call-start
  9.0 0.7 compare_select_fusion
  9.7 1.9 gather_fusion.2
  11.5 0.7 compare_and_fusion
  12.2 99.0 %all-gather.4.cloned.1.call-done = bf16[1,896,896]{2,0,1:T(2,128)(2,1)} async-done(((bf16[1,28,896]{2,0,1:T(2,128)(2,1)}), bf16[1,896,896]{2,0,1:T(2,128)(2,1)}) %all-gather.4.cloned.1.call-update) | async-done | bytes 1605648 | tf_op jit(solution)/shard_map/all_gather | solution.py:20
  111.2 3.0 fusion.16
  114.2 0.0 all-gather.6.cloned.1.call-update
  114.2 0.0 all-gather.8.cloned.1.call-start
  114.2 0.0 copy-done.5
  114.3 0.0 copy-done.1
  114.3 0.6 gather_fusion.3
  114.9 0.7 broadcast_select_fusion
  115.6 0.0 all-gather.8.cloned.1.call-update
  115.7 0.0 copy-done
  115.7 0.9 gather_fusion.1
  116.5 0.0 copy-start.2
  116.6 1.1 bitcast_select_fusion
  117.6 6.8 %all-to-all-start.1 = ((bf16[64,32,128]{2,0,1:T(8,128)(2,1)}), bf16[64,32,128]{2,0,1:T(8,128)(2,1)S(1)}, u32[]{:S(2)}, u32[]{:S(2)}) async-start(bf16[64,32,128]{2,0,1:T(8,128)(2,1)} %bitcast_select_fusion), calls=%async_computation.1 | async-start | bytes 1048576 | tf_op jit(solution)/shard_map/all_to_all | solution.py:33
  124.4 0.0 copy-start.3
  124.5 0.0 copy-start.4
  124.5 0.0 copy-start.6
  124.5 0.7 gather_fusion
  125.2 0.0 copy-done.2
  125.2 0.2 copy.23
  125.4 0.8 bitcast_select_fusion.1
  126.2 16.7 %all-to-all-done.1 = bf16[64,32,128]{2,0,1:T(8,128)(2,1)S(1)} async-done(((bf16[64,32,128]{2,0,1:T(8,128)(2,1)}), bf16[64,32,128]{2,0,1:T(8,128)(2,1)S(1)}, u32[]{:S(2)}, u32[]{:S(2)}) %all-to-all-start.1) | async-done | bytes 524320 | tf_op jit(solution)/shard_map/all_to_all | solution.py:33
  142.9 5.6 all-to-all-start
  148.6 0.0 all-reduce.2.cloned.1.call-start
  148.6 66.9 %all-gather.6.cloned.1.call-done = bf16[2048,896]{1,0:T(8,128)(2,1)} async-done(((bf16[64,896]{1,0:T(8,128)(2,1)}), bf16[2048,896]{1,0:T(8,128)(2,1)}) %all-gather.6.cloned.1.call-update) | async-done | bytes 3670032 | tf_op jit(solution)/shard_map/all_gather | solution.py:47
  215.6 3.0 fusion.13
  218.6 2.8 fusion.12
  221.4 78.9 %all-gather.8.cloned.1.call-done = bf16[1024,896]{1,0:T(8,128)(2,1)} async-done(((bf16[32,896]{1,0:T(8,128)(2,1)}), bf16[1024,896]{1,0:T(8,128)(2,1)}) %all-gather.8.cloned.1.call-update) | async-done | bytes 1835024 | tf_op jit(solution)/shard_map/all_gather | solution.py:82
  300.3 2.9 convolution_convert_fusion.2
  303.1 0.0 all-reduce.2.cloned.1.call-update
  303.2 0.0 reduce-scatter.2.cloned.1.call-start
  303.2 0.0 all-to-all-done
  303.2 1.9 convolution_convert_fusion.1
  305.1 0.0 reduce-scatter.2.cloned.1.call-update
  305.1 116.9 %all-reduce.2.cloned.1.call-done = bf16[32,32,128]{2,1,0:T(8,128)(2,1)} async-done(((bf16[32,32,128]{2,1,0:T(8,128)(2,1)}), bf16[32,32,128]{2,1,0:T(8,128)(2,1)}) %all-reduce.2.cloned.1.call-update) | async-done | bytes 262160 | tf_op jit(solution)/shard_map/psum | solution.py:87
  422.1 25.1 %all_to_all.48 = bf16[32,32,128]{2,1,0:T(8,128)(2,1)S(1)} all-to-all(bf16[32,32,128]{2,1,0:T(8,128)(2,1)} %all-reduce.2.cloned.1.call-done), channel_id=1, replica_groups=mesh['fsdp'=32,'tp'=16] {'fsdp'}, dimensions={0} | all-to-all | bytes 524288 | tf_op jit(solution)/shard_map/all_to_all | solution.py:88
  447.1 0.7 copy_bitcast_fusion
  447.8 212.5 %reduce-scatter.2.cloned.1.call-done = bf16[32,896]{1,0:T(8,128)(2,1)} async-done(((bf16[1024,896]{1,0:T(8,128)(2,1)}), bf16[32,896]{1,0:T(8,128)(2,1)}) %reduce-scatter.2.cloned.1.call-update) | async-done | bytes 57360 | tf_op jit(solution)/shard_map/reduce_scatter | solution.py:75
  (7 shorter events, 0.0 us)
Async XLA Ops:
  7.2 108.5 %copy-start = (bf16[256,4096]{1,0:T(8,128)(2,1)S(1)}, bf16[256,4096]{1,0:T(8,128)(2,1)}, u32[]{:S(2)}) copy-start(bf16[256,4096]{1,0:T(8,128)(2,1)} %param.9) | copy-start | bytes 6291460
  7.2 107.1 %copy-start.1 = (bf16[256,896]{1,0:T(8,128)(2,1)S(1)}, bf16[256,896]{1,0:T(8,128)(2,1)}, u32[]{:S(2)}) copy-start(bf16[256,896]{1,0:T(8,128)(2,1)} %param.10) | copy-start | bytes 1376260
  7.2 107.0 %copy-start.5 = (s32[32]{0:T(128)S(1)}, s32[32]{0:T(128)}, u32[]{:S(2)}) copy-start(s32[32]{0:T(128)} %param.17) | copy-start | bytes 388
  7.2 104.0 %all-gather.4.cloned.1.call-start = ((), (), s32[]{:S(2)}) async-start(), calls=%async_computation.4 | async-start | bytes 3311616 | tf_op jit(solution)/shard_map/all_gather | solution.py:20
  9.0 206.6 %all-gather.6.cloned.1.call-start = ((), (), s32[]{:S(2)}) async-start(), calls=%async_computation.5 | async-start | bytes 3784704 | tf_op jit(solution)/shard_map/all_gather | solution.py:47
  114.2 186.1 %all-gather.8.cloned.1.call-start = ((), (), s32[]{:S(2)}) async-start(), calls=%async_computation.7 | async-start | bytes 1892352 | tf_op jit(solution)/shard_map/all_gather | solution.py:82
  116.5 8.7 %copy-start.2 = (bf16[128,896]{1,0:T(8,128)(2,1)S(1)}, bf16[128,896]{1,0:T(8,128)(2,1)}, u32[]{:S(2)}) copy-start(bf16[128,896]{1,0:T(8,128)(2,1)} %param.11) | copy-start | bytes 688132
  117.6 25.3 %all-to-all-start.1 = ((bf16[64,32,128]{2,0,1:T(8,128)(2,1)}), bf16[64,32,128]{2,0,1:T(8,128)(2,1)S(1)}, u32[]{:S(2)}, u32[]{:S(2)}) async-start(bf16[64,32,128]{2,0,1:T(8,128)(2,1)} %bitcast_select_fusion), calls=%async_computation.1 | async-start | bytes 1048576 | tf_op jit(solution)/shard_map/all_to_all | solution.py:33
  124.4 91.1 %copy-start.3 = (bf16[1,128,128]{2,1,0:T(8,128)(2,1)S(1)}, bf16[1,128,128]{2,1,0:T(8,128)(2,1)}, u32[]{:S(2)}) copy-start(bf16[1,128,128]{2,1,0:T(8,128)(2,1)} %param.12) | copy-start | bytes 98308
  124.5 91.1 %copy-start.4 = (f32[896]{0:T(1024)S(1)}, f32[896]{0:T(1024)}, u32[]{:S(2)}) copy-start(f32[896]{0:T(1024)} %param.15) | copy-start | bytes 10756
  124.5 91.1 %copy-start.6 = (f32[128]{0:T(128)S(1)}, f32[128]{0:T(128)}, u32[]{:S(2)}) copy-start(f32[128]{0:T(128)} %param.14) | copy-start | bytes 1540
  142.9 160.3 %all-to-all-start = ((bf16[32,32,128]{2,0,1:T(8,128)(2,1)}), bf16[32,32,128]{2,0,1:T(8,128)(2,1)S(1)}, u32[]{:S(2)}, u32[]{:S(2)}) async-start(bf16[32,32,128]{2,0,1:T(8,128)(2,1)} %bitcast_select_fusion.1), calls=%async_computation | async-start | bytes 524288 | tf_op jit(solution)/shard_map/all_to_all | solution.py:74
  148.6 273.5 %all-reduce.2.cloned.1.call-start = ((), (), s32[]{:S(2)}) async-start(), calls=%async_computation.8 | async-start | bytes 524288 | tf_op jit(solution)/shard_map/psum | solution.py:87
  303.2 357.2 %reduce-scatter.2.cloned.1.call-start = ((), (), s32[]{:S(2)}) async-start(), calls=%async_computation.6 | async-start | bytes 1892352 | tf_op jit(solution)/shard_map/reduce_scatter | solution.py:75
Sparse Core Ops, SparseCore 0:
  11.7 99.4 all-gather.3
  114.4 101.1 all-gather.5
  219.3 80.9 all-gather.7
  303.3 118.7 all-reduce.1
  427.6 232.6 reduce-scatter.1
where the time goes:
time: 667 us
  waiting for transfers between devices  591 us (89%)
  blocking collectives  25.1 us (4%)
  between operations  14 us (2%)
  matrix products  13.6 us (2%)
  starting transfers between devices  12.7 us (2%)
  local copies, waits for them, and re-layouts  6.69 us (1%)
    reduce_scatter x1, waiting for transfers between devices, shards(): lax.psum_scatter(jnp.dot(retain_cols, new_weight, preferred_element_type=...  213 us
    psum x1, waiting for transfers between devices, shards(): grad_summed = lax.psum(grad_cols.astype(jnp.bfloat16), 'tp')  117 us
    all_gather x1, waiting for transfers between devices, shards(): basis_full = lax.all_gather(basis_out, 'fsdp', axis=1, tiled=True)  99 us
    all_gather x1, waiting for transfers between devices, shards(): lax.all_gather(retain_cots, 'fsdp', axis=0, tiled=True)  78.9 us
    all_gather x1, waiting for transfers between devices, shards(): lax.all_gather(rotated_cots, 'fsdp', axis=0, tiled=True)  66.9 us
    all_to_all x1, blocking collectives, shards(): lax.all_to_all(grad_summed, 'fsdp', split_axis=0, concat_axis=1, tiled=True)  25.1 us
    all_to_all x1, waiting for transfers between devices, shards(): lax.all_to_all(forget_acts, 'fsdp', split_axis=1, concat_axis=0, tiled=True)  16.7 us
  transfers between devices with their start and end apart: 7, of which 6 were waited for; matrix products, arithmetic and copies ran while one was open for 3% of the time, Pallas kernels for 0%

commit v1 on v0

--- a/solution.py
+++ b/solution.py
@@ -85,7 +85,12 @@
         preferred_element_type=jnp.float32,
     )
     grad_summed = lax.psum(grad_cols.astype(jnp.bfloat16), "tp")
-    back_grads = lax.all_to_all(grad_summed, "fsdp", split_axis=0, concat_axis=1, tiled=True)
+    back_grads = jnp.concatenate(
+        lax.all_to_all(
+            jnp.stack(jnp.split(grad_summed, lax.axis_size("fsdp"), axis=0)), "fsdp", 0, 0
+        ),
+        axis=1,
+    )
     return (retained, back_grads)
 
 

time: 667 us -> 670 us (level)
  local copies, waits for them, and re-layouts: 6.69 us -> 29.2 us
  waiting for transfers between devices: 591 us -> 569 us
    reduce_scatter x1, waiting for transfers between devices: 213 us -> 191 us  [shards(): lax.psum_scatter(jnp.dot(retain_cols, new_weight, preferred_element_type=...]
    unnamed x16 -> x47, local copies, waits for them, and re-layouts: 1.9 us -> 23.7 us
  transfers between devices with their start and end apart: 7 -> 7, of which waited for: 6 -> 6; matrix products, arithmetic and copies ran while one was open for 3% -> 6% of each run, Pallas kernels for 0% -> 0%
where the time goes in v1:
time: 670 us; the launch traced here: 668 us
  waiting for transfers between devices  569 us (85%)
  local copies, waits for them, and re-layouts  29.2 us (4%)
  blocking collectives  25.2 us (4%)
  between operations  14 us (2%)
  matrix products  13.6 us (2%)
  starting transfers between devices  12.7 us (2%)
    reduce_scatter x1, waiting for transfers between devices, shards(): lax.psum_scatter(jnp.dot(retain_cols, new_weight, preferred_element_type=...  191 us
    psum x1, waiting for transfers between devices, shards(): grad_summed = lax.psum(grad_cols.astype(jnp.bfloat16), 'tp')  117 us
    all_gather x1, waiting for transfers between devices, shards(): basis_full = lax.all_gather(basis_out, 'fsdp', axis=1, tiled=True)  99 us
    all_gather x1, waiting for transfers between devices, shards(): lax.all_gather(retain_cots, 'fsdp', axis=0, tiled=True)  78.9 us
    all_gather x1, waiting for transfers between devices, shards(): lax.all_gather(rotated_cots, 'fsdp', axis=0, tiled=True)  66.9 us
    all_to_all x1, blocking collectives, shards(): lax.all_to_all(jnp.stack(jnp.split(grad_summed, lax.axis_size('fsdp'), ax...  25.2 us
    unnamed x47, local copies, waits for them, and re-layouts  23.7 us
    all_to_all x1, waiting for transfers between devices, shards(): lax.all_to_all(forget_acts, 'fsdp', split_axis=1, concat_axis=0, tiled=True)  16.7 us
  transfers between devices with their start and end apart: 7, of which 6 were waited for; matrix products, arithmetic and copies ran while one was open for 6% of the time, Pallas kernels for 0%

profile of v1, /device:TPU:2, one launch (start us, length us, event | category | flops | bytes accessed | tf_op | source)
XLA Modules:
  0.0 667.7 jit_solution(9526452176423979905)
XLA Ops:
  7.2 1.7 copy.24
  9.7 1.9 gather_fusion.2
  12.2 99.0 %all-gather.4.cloned.1.call-done = bf16[1,896,896]{2,0,1:T(2,128)(2,1)} async-done(((bf16[1,28,896]{2,0,1:T(2,128)(2,1)}), bf16[1,896,896]{2,0,1:T(2,128)(2,1)}) %all-gather.4.cloned.1.call-update) | async-done | bytes 1605648 | tf_op jit(solution)/shard_map/all_gather | solution.py:20
  111.2 3.0 fusion.16
  114.9 0.7 broadcast_select_fusion
  115.7 0.9 gather_fusion.1
  116.6 1.1 bitcast_select_fusion
  117.6 6.8 %all-to-all-start.1 = ((bf16[64,32,128]{2,0,1:T(8,128)(2,1)}), bf16[64,32,128]{2,0,1:T(8,128)(2,1)S(1)}, u32[]{:S(2)}, u32[]{:S(2)}) async-start(bf16[64,32,128]{2,0,1:T(8,128)(2,1)} %bitcast_select_fusion), calls=%async_computation.1 | async-start | bytes 1048576 | tf_op jit(solution)/shard_map/all_to_all | solution.py:33
  124.5 0.7 gather_fusion
  125.4 0.8 bitcast_select_fusion.1
  126.2 16.7 %all-to-all-done.1 = bf16[64,32,128]{2,0,1:T(8,128)(2,1)S(1)} async-done(((bf16[64,32,128]{2,0,1:T(8,128)(2,1)}), bf16[64,32,128]{2,0,1:T(8,128)(2,1)S(1)}, u32[]{:S(2)}, u32[]{:S(2)}) %all-to-all-start.1) | async-done | bytes 524320 | tf_op jit(solution)/shard_map/all_to_all | solution.py:33
  142.9 5.6 all-to-all-start
  148.6 66.9 %all-gather.6.cloned.1.call-done = bf16[2048,896]{1,0:T(8,128)(2,1)} async-done(((bf16[64,896]{1,0:T(8,128)(2,1)}), bf16[2048,896]{1,0:T(8,128)(2,1)}) %all-gather.6.cloned.1.call-update) | async-done | bytes 3670032 | tf_op jit(solution)/shard_map/all_gather | solution.py:47
  215.6 3.0 fusion.13
  218.6 2.8 fusion.12
  221.4 78.9 %all-gather.8.cloned.1.call-done = bf16[1024,896]{1,0:T(8,128)(2,1)} async-done(((bf16[32,896]{1,0:T(8,128)(2,1)}), bf16[1024,896]{1,0:T(8,128)(2,1)}) %all-gather.8.cloned.1.call-update) | async-done | bytes 1835024 | tf_op jit(solution)/shard_map/all_gather | solution.py:82
  300.3 2.9 convolution_convert_fusion.2
  303.2 1.9 convolution_convert_fusion.1
  305.1 116.9 %all-reduce.2.cloned.1.call-done = bf16[1024,128]{1,0:T(8,128)(2,1)} async-done(((bf16[1024,128]{1,0:T(8,128)(2,1)}), bf16[1024,128]{1,0:T(8,128)(2,1)}) %all-reduce.2.cloned.1.call-update) | async-done | bytes 262160 | tf_op jit(solution)/shard_map/psum | solution.py:87
  422.8 0.7 constant_dynamic-update-slice_fusion.30
  423.5 0.7 constant_dynamic-update-slice_fusion.29
  424.9 0.7 constant_dynamic-update-slice_fusion.27
  425.6 0.7 constant_dynamic-update-slice_fusion.26
  426.3 0.7 constant_dynamic-update-slice_fusion.25
  427.0 0.7 constant_dynamic-update-slice_fusion.24
  428.4 0.7 constant_dynamic-update-slice_fusion.22
  429.1 0.7 constant_dynamic-update-slice_fusion.21
  429.8 0.7 constant_dynamic-update-slice_fusion.20
  430.5 0.7 constant_dynamic-update-slice_fusion.19
  431.2 0.7 constant_dynamic-update-slice_fusion.18
  431.9 0.7 constant_dynamic-update-slice_fusion.17
  432.6 0.7 constant_dynamic-update-slice_fusion.16
  433.3 0.7 constant_dynamic-update-slice_fusion.15
  434.0 0.7 constant_dynamic-update-slice_fusion.14
  434.7 0.7 constant_dynamic-update-slice_fusion.13
  435.4 0.7 constant_dynamic-update-slice_fusion.12
  436.1 0.7 constant_dynamic-update-slice_fusion.11
  436.8 0.7 constant_dynamic-update-slice_fusion.10
  438.2 0.7 constant_dynamic-update-slice_fusion.8
  438.9 0.7 constant_dynamic-update-slice_fusion.7
  439.6 0.7 constant_dynamic-update-slice_fusion.6
  440.3 0.7 constant_dynamic-update-slice_fusion.5
  441.8 0.7 constant_dynamic-update-slice_fusion.3
  442.5 0.7 constant_dynamic-update-slice_fusion.2
  443.2 0.7 constant_dynamic-update-slice_fusion.1
  444.6 25.2 %all_to_all.34 = bf16[32,32,128]{2,1,0:T(8,128)(2,1)S(1)} all-to-all(bf16[32,32,128]{2,1,0:T(8,128)(2,1)S(1)} %constant_dynamic-update-slice_fusion), channel_id=1, replica_groups=mesh['fsdp'=32,'tp'=16] {'fsdp'}, dimensions={0} | all-to-all | bytes 524288 | tf_op jit(solution)/shard_map/all_to_all | solution.py:89
  469.7 0.7 copy_bitcast_fusion
  470.4 190.7 %reduce-scatter.2.cloned.1.call-done = bf16[32,896]{1,0:T(8,128)(2,1)} async-done(((bf16[1024,896]{1,0:T(8,128)(2,1)}), bf16[32,896]{1,0:T(8,128)(2,1)}) %reduce-scatter.2.cloned.1.call-update) | async-done | bytes 57360 | tf_op jit(solution)/shard_map/reduce_scatter | solution.py:75
  (39 shorter events, 6.7 us)
Async XLA Ops:
  7.2 108.5 %copy-start = (bf16[256,4096]{1,0:T(8,128)(2,1)S(1)}, bf16[256,4096]{1,0:T(8,128)(2,1)}, u32[]{:S(2)}) copy-start(bf16[256,4096]{1,0:T(8,128)(2,1)} %param.9) | copy-start | bytes 6291460
  7.2 107.1 %copy-start.1 = (bf16[256,896]{1,0:T(8,128)(2,1)S(1)}, bf16[256,896]{1,0:T(8,128)(2,1)}, u32[]{:S(2)}) copy-start(bf16[256,896]{1,0:T(8,128)(2,1)} %param.10) | copy-start | bytes 1376260
  7.2 107.0 %copy-start.5 = (s32[32]{0:T(128)S(1)}, s32[32]{0:T(128)}, u32[]{:S(2)}) copy-start(s32[32]{0:T(128)} %param.17) | copy-start | bytes 388
  7.2 104.0 %all-gather.4.cloned.1.call-start = ((), (), s32[]{:S(2)}) async-start(), calls=%async_computation.4 | async-start | bytes 3311616 | tf_op jit(solution)/shard_map/all_gather | solution.py:20
  9.0 206.6 %all-gather.6.cloned.1.call-start = ((), (), s32[]{:S(2)}) async-start(), calls=%async_computation.5 | async-start | bytes 3784704 | tf_op jit(solution)/shard_map/all_gather | solution.py:47
  114.2 186.1 %all-gather.8.cloned.1.call-start = ((), (), s32[]{:S(2)}) async-start(), calls=%async_computation.7 | async-start | bytes 1892352 | tf_op jit(solution)/shard_map/all_gather | solution.py:82
  116.5 8.7 %copy-start.2 = (bf16[128,896]{1,0:T(8,128)(2,1)S(1)}, bf16[128,896]{1,0:T(8,128)(2,1)}, u32[]{:S(2)}) copy-start(bf16[128,896]{1,0:T(8,128)(2,1)} %param.11) | copy-start | bytes 688132
  117.6 25.3 %all-to-all-start.1 = ((bf16[64,32,128]{2,0,1:T(8,128)(2,1)}), bf16[64,32,128]{2,0,1:T(8,128)(2,1)S(1)}, u32[]{:S(2)}, u32[]{:S(2)}) async-start(bf16[64,32,128]{2,0,1:T(8,128)(2,1)} %bitcast_select_fusion), calls=%async_computation.1 | async-start | bytes 1048576 | tf_op jit(solution)/shard_map/all_to_all | solution.py:33
  124.4 91.1 %copy-start.3 = (bf16[1,128,128]{2,1,0:T(8,128)(2,1)S(1)}, bf16[1,128,128]{2,1,0:T(8,128)(2,1)}, u32[]{:S(2)}) copy-start(bf16[1,128,128]{2,1,0:T(8,128)(2,1)} %param.12) | copy-start | bytes 98308
  124.5 91.1 %copy-start.4 = (f32[896]{0:T(1024)S(1)}, f32[896]{0:T(1024)}, u32[]{:S(2)}) copy-start(f32[896]{0:T(1024)} %param.15) | copy-start | bytes 10756
  124.5 91.1 %copy-start.6 = (f32[128]{0:T(128)S(1)}, f32[128]{0:T(128)}, u32[]{:S(2)}) copy-start(f32[128]{0:T(128)} %param.14) | copy-start | bytes 1540
  142.9 160.3 %all-to-all-start = ((bf16[32,32,128]{2,0,1:T(8,128)(2,1)}), bf16[32,32,128]{2,0,1:T(8,128)(2,1)S(1)}, u32[]{:S(2)}, u32[]{:S(2)}) async-start(bf16[32,32,128]{2,0,1:T(8,128)(2,1)} %bitcast_select_fusion.1), calls=%async_computation | async-start | bytes 524288 | tf_op jit(solution)/shard_map/all_to_all | solution.py:74
  148.6 273.5 %all-reduce.2.cloned.1.call-start = ((), (), s32[]{:S(2)}) async-start(), calls=%async_computation.8 | async-start | bytes 524288 | tf_op jit(solution)/shard_map/psum | solution.py:87
  303.2 358.0 %reduce-scatter.2.cloned.1.call-start = ((), (), s32[]{:S(2)}) async-start(), calls=%async_computation.6 | async-start | bytes 1892352 | tf_op jit(solution)/shard_map/reduce_scatter | solution.py:75
Sparse Core Ops, SparseCore 0:
  11.7 99.4 all-gather.3
  114.4 101.1 all-gather.5
  219.3 80.9 all-gather.7
  303.3 118.7 all-reduce.1
  427.6 233.4 reduce-scatter.1
